TPU v7x, 32 devices: a whole 2x2x4 slice. The times are simulated.
32 devices in a mesh: groups: 2 (over y), rows: 4 (over z), sub: 4 (over x, core).
Axes of the slice: x: 2, y: 2, z: 4, core: 2. Of those that a mesh axis runs over, the one named last changes fastest.
Arguments:
- embeddings: bfloat16 [8192, 1024], P(('groups', 'rows', 'sub')), parts along dimension 0, may hold values from -4 to 4
- pivots: int32 [4, 256], P('groups'), parts along dimension 0, may hold values from 0 to 4095, as said below
Outputs:
- whitened: float32 [8192, 512], P(('groups', 'rows', 'sub')), parts along dimension 0
There are 2 independent parts, one for each index of `groups`. A program takes and returns all parts, laid end to end along the dimension named above; each array names one. Nothing has to cross between parts.
Inputs may be any that keep to these rules, and one draw needn't show every extreme that they name: `pivots`: the 512 pivot indices are all different.
All inputs are finite; a program needn't handle non-finite values.
Results may differ from a plain program's by a relative error of at most 0.0003.
Values may be sent and summed in bfloat16 or wider, within the bound.
A program may use at most 64 MiB of HBM per device.

v0:
```python
import jax
import jax.numpy as jnp
from jax import lax
from jax.sharding import PartitionSpec as P

ridge_shift = 0.001
floor_value = -1e30


def squares(points):
    return jnp.sum(jnp.square(points.astype(jnp.float32)), axis=1)


def kernel_tile(points, point_sq, others, other_sq):
    products = lax.dot_general(
        points, others, (((1,), (1,)), ((), ())), preferred_element_type=jnp.float32
    )
    return jnp.exp((2.0 * products - point_sq[:, None] - other_sq[None, :]) / points.shape[1])


def times_transposed(first_set, second_set):
    return lax.dot_general(
        first_set,
        second_set,
        (((1,), (1,)), ((), ())),
        precision=lax.Precision.HIGHEST,
        preferred_element_type=jnp.float32,
    )


def lower_inverse(matrix):
    cholesky_low = jnp.linalg.cholesky(matrix)
    identity = jnp.eye(matrix.shape[0], dtype=jnp.float32)
    return jax.scipy.linalg.solve_triangular(cholesky_low, identity, lower=True)


def owners_pick(source, indices, first_row, fill_value):
    local_spot = indices - first_row
    owned_mask = (local_spot >= 0) & (local_spot < source.shape[0])
    local_spot = jnp.clip(local_spot, 0, source.shape[0] - 1)
    picked = jnp.take(source, local_spot, axis=0)
    return jnp.where(owned_mask[:, None], picked, jnp.asarray(fill_value, source.dtype))


def on_device(embeddings, pivots):
    local_count = embeddings.shape[0]
    devices = lax.axis_size(("rows", "sub"))
    first_row = lax.axis_index(("rows", "sub")) * local_count
    blocks = pivots.shape[0]
    norms = squares(embeddings)
    factor = jnp.zeros((local_count, 0), jnp.float32)
    for section in range(blocks):
        piv_rows = lax.pmax(
            owners_pick(embeddings, pivots[section], first_row, floor_value), ("rows", "sub")
        )
        if section > 0:
            piv_factor = lax.pmax(
                owners_pick(factor, pivots[section], first_row, floor_value), ("rows", "sub")
            )
        piv_sq = squares(piv_rows)
        residual = kernel_tile(embeddings, norms, piv_rows, piv_sq)
        pivot_gram = kernel_tile(piv_rows, piv_sq, piv_rows, piv_sq)
        if section > 0:
            residual = residual - times_transposed(factor, piv_factor)
            pivot_gram = pivot_gram - times_transposed(piv_factor, piv_factor)
        inverse = lower_inverse(pivot_gram)
        factor = jnp.concatenate([factor, times_transposed(residual, inverse)], axis=1)
    feature_count = factor.shape[1]
    gram_share = lax.psum_scatter(
        lax.dot_general(
            factor,
            factor,
            (((0,), (0,)), ((), ())),
            precision=lax.Precision.HIGHEST,
            preferred_element_type=jnp.float32,
        ),
        ("rows", "sub"),
        scatter_dimension=0,
        tiled=True,
    )
    gram_sum = lax.all_gather(gram_share, ("rows", "sub"), axis=0, tiled=True)
    point_total = local_count * devices
    gram_sum = gram_sum / point_total + ridge_shift * jnp.eye(feature_count, dtype=jnp.float32)
    return times_transposed(factor, lower_inverse(gram_sum))


def solution(mesh):
    return jax.shard_map(
        on_device,
        mesh=mesh,
        in_specs=(P(("groups", "rows", "sub"), None), P("groups", None)),
        out_specs=P(("groups", "rows", "sub"), None),
        check_vma=False,
    )
```

profile of v0, /device:TPU:0, one launch (start us, length us, event | category | flops | bytes accessed | tf_op | source)
XLA Modules:
  0.0 583.5 jit_solution(17623190636720332180)
XLA Ops:
  7.3 2.7 gather_fusion.2
  14.0 96.1 %all-reduce.8.cloned.1.call-done = (bf16[256,1024]{1,0:T(8,128)(2,1)}, bf16[256,1024]{1,0:T(8,128)(2,1)}) async-done(((bf16[256,1024]{1,0:T(8,128)(2,1)}, bf16[256,1024]{1,0:T(8,128)(2,1)}), (bf16[256,1024]{1,0:T(8,128)(2,1)}, bf16[256,1024]{1,0:T(8,128)(2,1)})) %all-reduce.8.cloned.1.call-update) | async-done | bytes 1048592 | tf_op jit(solution)/shard_map/pmax | solution.py:53
  112.0 11.7 %cholesky.354 = f32[128,128]{1,0:T(8,128)S(1)} custom-call(f32[128,128]{1,0:T(8,128)S(1)} %cholesky.404), custom_call_target="Cholesky" | custom-call | tf_op jit(solution)/shard_map/jit(cholesky)/cholesky | solution.py:32
  123.7 9.8 %custom-call.44 = f32[1,128,128]{1,2,0:T(8,128)S(1)} custom-call(f32[1,128,128]{2,1,0:T(8,128)S(1)} %get-tuple-element.94), custom_call_target="InvertDiagBlocksLowerTriangular" | custom-call | tf_op jit(solution)/shard_map/jit(cholesky)/cholesky/custom-call.8 | solution.py:32
  134.0 11.7 %cholesky.364 = f32[128,128]{1,0:T(8,128)S(1)} custom-call(f32[128,128]{1,0:T(8,128)S(1)} %convolution_subtract_fusion.10), custom_call_target="Cholesky" | custom-call | tf_op jit(solution)/shard_map/jit(cholesky)/cholesky | solution.py:32
  148.6 4.3 while.6
  149.4 1.4 bitcast_dynamic-update-slice_fusion.7
  151.5 1.4 bitcast_dynamic-update-slice_fusion.7
  152.9 19.7 %custom-call.45 = f32[2,128,128]{1,2,0:T(8,128)S(1)} custom-call(f32[2,128,128]{2,1,0:T(8,128)S(1)} %get-tuple-element.31), custom_call_target="InvertDiagBlocksLowerTriangular" | custom-call | tf_op jit(solution)/shard_map/jit(_solve_triangular)/triangular_solve | solution.py:34
  177.3 87.3 %all-reduce.6.cloned.1.call-done = f32[256,256]{1,0:T(8,128)} async-done(((f32[256,256]{1,0:T(8,128)}), f32[256,256]{1,0:T(8,128)}) %all-reduce.6.cloned.1.call-update) | async-done | bytes 262160 | tf_op jit(solution)/shard_map/pmax | solution.py:57
  264.6 1.4 convolution_subtract_fusion.2
  266.2 11.7 %cholesky.381 = f32[128,128]{1,0:T(8,128)S(1)} custom-call(f32[128,128]{1,0:T(8,128)S(1)} %cholesky.407), custom_call_target="Cholesky" | custom-call | tf_op jit(solution)/shard_map/jit(cholesky)/cholesky | solution.py:32
  278.0 9.8 %custom-call.46 = f32[1,128,128]{1,2,0:T(8,128)S(1)} custom-call(f32[1,128,128]{2,1,0:T(8,128)S(1)} %get-tuple-element.90), custom_call_target="InvertDiagBlocksLowerTriangular" | custom-call | tf_op jit(solution)/shard_map/jit(cholesky)/cholesky/custom-call.8 | solution.py:32
  288.3 11.7 %cholesky.391 = f32[128,128]{1,0:T(8,128)S(1)} custom-call(f32[128,128]{1,0:T(8,128)S(1)} %convolution_subtract_fusion.9), custom_call_target="Cholesky" | custom-call | tf_op jit(solution)/shard_map/jit(cholesky)/cholesky | solution.py:32
  302.8 4.5 while.7
  303.8 1.4 bitcast_dynamic-update-slice_fusion.8
  307.3 19.7 %custom-call.47 = f32[2,128,128]{1,2,0:T(8,128)S(1)} custom-call(f32[2,128,128]{2,1,0:T(8,128)S(1)} %get-tuple-element.32), custom_call_target="InvertDiagBlocksLowerTriangular" | custom-call | tf_op jit(solution)/shard_map/jit(_solve_triangular)/triangular_solve | solution.py:34
  330.3 2.0 fusion.36
  332.4 58.0 %reduce-scatter.4.cloned.1.call-done = f32[32,512]{1,0:T(8,128)} async-done(((f32[512,512]{1,0:T(8,128)}), f32[32,512]{1,0:T(8,128)}) %reduce-scatter.4.cloned.1.call-update) | async-done | bytes 65552 | tf_op jit(solution)/shard_map/reduce_scatter | solution.py:69
  392.3 37.3 %all-gather.2.cloned.1.call-done = f32[512,512]{1,0:T(8,128)} async-done(((f32[32,512]{1,0:T(8,128)}), f32[512,512]{1,0:T(8,128)}) %all-gather.2.cloned.1.call-update) | async-done | bytes 1048592 | tf_op jit(solution)/shard_map/all_gather | solution.py:81
  429.6 1.6 copy.49
  431.9 11.7 %cholesky.166 = f32[128,128]{1,0:T(8,128)S(1)} custom-call(f32[128,128]{1,0:T(8,128)S(1)} %cholesky.410), custom_call_target="Cholesky" | custom-call | tf_op jit(solution)/shard_map/jit(cholesky)/cholesky | solution.py:32
  443.7 9.8 %custom-call.36 = f32[1,128,128]{1,2,0:T(8,128)S(1)} custom-call(f32[1,128,128]{2,1,0:T(8,128)S(1)} %get-tuple-element.86), custom_call_target="InvertDiagBlocksLowerTriangular" | custom-call | tf_op jit(solution)/shard_map/jit(cholesky)/cholesky | solution.py:32
  454.2 11.7 %cholesky.189 = f32[128,128]{1,0:T(8,128)S(1)} custom-call(f32[128,128]{1,0:T(8,128)S(1)} %cholesky.414), custom_call_target="Cholesky" | custom-call | tf_op jit(solution)/shard_map/jit(cholesky)/cholesky | solution.py:32
  466.2 9.9 %custom-call.37 = f32[1,128,128]{1,2,0:T(8,128)S(1)} custom-call(f32[1,128,128]{2,1,0:T(8,128)S(1)} %get-tuple-element.84), custom_call_target="InvertDiagBlocksLowerTriangular" | custom-call | tf_op jit(solution)/shard_map/jit(cholesky)/cholesky | solution.py:32
  477.3 11.7 %cholesky.292 = f32[128,128]{1,0:T(8,128)S(1)} custom-call(f32[128,128]{1,0:T(8,128)S(1)} %cholesky.419), custom_call_target="Cholesky" | custom-call | tf_op jit(solution)/shard_map/jit(cholesky)/cholesky | solution.py:32
  489.1 9.8 %custom-call.48 = f32[1,128,128]{1,2,0:T(8,128)S(1)} custom-call(f32[1,128,128]{2,1,0:T(8,128)S(1)} %get-tuple-element.82), custom_call_target="InvertDiagBlocksLowerTriangular" | custom-call | tf_op jit(solution)/shard_map/jit(cholesky)/cholesky/custom-call.8 | solution.py:32
  499.7 11.9 %cholesky.305 = f32[128,128]{1,0:T(8,128)S(1)} custom-call(f32[128,128]{1,0:T(8,128)S(1)} %convolution_subtract_fusion.11), custom_call_target="Cholesky" | custom-call | tf_op jit(solution)/shard_map/jit(cholesky)/cholesky | solution.py:32
  517.1 10.9 %while.5 = (s32[]{:T(128)}, f32[512,512]{0,1:T(8,128)S(1)}, s32[4,2]{0,1:T(2,128)S(1)}, f32[4,128,128]{2,1,0:T(8,128)}, s32[]{:T(128)}) while((s32[]{:T(128)}, f32[512,512]{0,1:T(8,128)S(1)}, s32[4,2]{0,1:T(2,128)S(1)}, f32[4,128,128]{2,1,0:T(8,128)}, s32[]{:T(128)}) %tuple.74), condition=%wide.while_cond.1, body=%wide.while_body.1.sunk | while | flops 2 | bytes 393829 | solution.py:34
  528.0 40.1 %custom-call.38 = f32[4,128,128]{1,2,0:T(8,128)S(1)} custom-call(f32[4,128,128]{2,1,0:T(8,128)} %get-tuple-element.24), custom_call_target="InvertDiagBlocksLowerTriangular" | custom-call | tf_op jit(solution)/shard_map/jit(_solve_triangular)/triangular_solve | solution.py:34
  571.7 1.5 convolution_subtract_fusion.4
  574.1 2.7 fusion.18
  (152 shorter events, 46.2 us)
Async XLA Ops:
  6.5 103.6 %all-reduce.8.cloned.1.call-start = ((), (), s32[]{:S(2)}) async-start(), calls=%async_computation.4 | async-start | bytes 2097152 | tf_op jit(solution)/shard_map/pmax | solution.py:53
  6.5 0.7 copy-start.7
  7.3 2.8 copy-start
  13.2 251.4 %all-reduce.6.cloned.1.call-start = ((), (), s32[]{:S(2)}) async-start(), calls=%async_computation.1 | async-start | bytes 524288 | tf_op jit(solution)/shard_map/pmax | solution.py:57
  110.1 1.3 copy-start.6
  175.4 1.0 copy-start.5
  176.2 214.2 %reduce-scatter.4.cloned.1.call-start = ((), (), s32[]{:S(2)}) async-start(), calls=%async_computation.3 | async-start | bytes 1114112 | tf_op jit(solution)/shard_map/reduce_scatter | solution.py:69
  327.6 1.0 copy-start.2
  329.6 0.7 copy-start.3
  332.4 97.3 %all-gather.2.cloned.1.call-start = ((), (), s32[]{:S(2)}) async-start(), calls=%async_computation.2 | async-start | bytes 1114112 | tf_op jit(solution)/shard_map/all_gather | solution.py:81
  517.0 52.3 %copy-start.1 = (f32[512,512]{0,1:T(8,128)S(1)}, f32[512,512]{0,1:T(8,128)}, u32[]{:S(2)}) copy-start(f32[512,512]{0,1:T(8,128)} %fusion.32) | copy-start | bytes 3145732
  573.2 1.0 copy-start.4
Sparse Core Ops, SparseCore 0:
  13.3 96.7 all-reduce.7
  176.4 88.1 all-reduce.5
  332.5 57.8 reduce-scatter.3
  392.6 36.9 all-gather.1
where the time goes:
time: 592 us; the launch traced here: 584 us
  waiting for transfers between devices  279 us (47%)
  other arithmetic  235 us (40%)
  local copies, waits for them, and re-layouts  29.6 us (5%)
  matrix products  19.4 us (3%)
  between operations  19.2 us (3%)
    another operation x29, other arithmetic, lower_inverse(): cholesky_low = jnp.linalg.cholesky(matrix)  149 us
    pmax x1, waiting for transfers between devices, on_device(): lax.pmax(owners_pick(embeddings, pivots[section], first_row, floor_value)...  96.1 us
    pmax x1, waiting for transfers between devices, on_device(): lax.pmax(owners_pick(factor, pivots[section], first_row, floor_value), ('...  87.3 us
    another operation x8, other arithmetic, lower_inverse(): return jax.scipy.linalg.solve_triangular(cholesky_low, identity, lower=True)  79.7 us
    reduce_scatter x1, waiting for transfers between devices, on_device(): lax.psum_scatter(lax.dot_general(factor, factor, (((0,), (0,)), ((), ()))...  58 us
    all_gather x1, waiting for transfers between devices, on_device(): gram_sum = lax.all_gather(gram_share, ('rows', 'sub'), axis=0, tiled=True)  37.3 us
  transfers between devices with their start and end apart: 4, of which 4 were waited for; matrix products, arithmetic and copies ran while one was open for 1% of the time, Pallas kernels for 0%

commit v1 on v0

v1 whole, which is shorter than its diff:
```python
import jax
import jax.numpy as jnp
from jax import lax
from jax.sharding import PartitionSpec as P

ridge_shift = 0.001
EXACT = lax.Precision.HIGHEST


def squares(points):
    return jnp.sum(jnp.square(points.astype(jnp.float32)), axis=1)


def kernel_tile(points, point_sq, others, other_sq):
    products = lax.dot_general(
        points, others, (((1,), (1,)), ((), ())), preferred_element_type=jnp.float32
    )
    return jnp.exp((2.0 * products - point_sq[:, None] - other_sq[None, :]) / points.shape[1])


def lower_inverse(matrix):
    cholesky_low = jnp.linalg.cholesky(matrix)
    identity = jnp.eye(matrix.shape[0], dtype=jnp.float32)
    return jax.scipy.linalg.solve_triangular(cholesky_low, identity, lower=True)


def on_device(embeddings, pivots):
    local_count, width = embeddings.shape
    devices = lax.axis_size(("rows", "sub"))
    first_row = lax.axis_index(("rows", "sub")) * local_count
    spots = pivots.reshape(-1) - first_row
    chosen = (spots[:, None] == lax.iota(jnp.int32, local_count)[None, :]).astype(jnp.bfloat16)
    mine = jnp.dot(chosen, embeddings, preferred_element_type=jnp.float32).astype(jnp.bfloat16)
    piv_rows = lax.psum(mine, ("rows", "sub"))
    norms = squares(embeddings)
    piv_sq = squares(piv_rows)
    tile = kernel_tile(embeddings, norms, piv_rows, piv_sq)
    gram = lax.psum(
        lax.dot_general(tile, tile, (((0,), (0,)), ((), ())), precision=EXACT), ("rows", "sub")
    )
    pivot_gram = kernel_tile(piv_rows, piv_sq, piv_rows, piv_sq)
    mixed = gram / (local_count * devices) + ridge_shift * pivot_gram
    return lax.dot_general(
        tile, lower_inverse(mixed), (((1,), (1,)), ((), ())), precision=EXACT
    )


def solution(mesh):
    return jax.shard_map(
        on_device,
        mesh=mesh,
        in_specs=(P(("groups", "rows", "sub"), None), P("groups", None)),
        out_specs=P(("groups", "rows", "sub"), None),
        check_vma=False,
    )
```

time: 592 us -> 356 us (0.60); the launches traced: 584 us -> 356 us
  other arithmetic: 235 us -> 123 us
  waiting for transfers between devices: 279 us -> 188 us
  local copies, waits for them, and re-layouts: 29.6 us -> 12.8 us
    psum x0 -> x2, waiting for transfers between devices: none -> 188 us  [the longest x1 96.8 us: on_device(): piv_rows = lax.psum(mine, ('rows', 'sub'))]
    pmax x2 -> x0, waiting for transfers between devices: 183 us -> none  [the longest x1 96.1 us: on_device(): lax.pmax(owners_pick(embeddings, pivots[section], first_row, floor_value)...]
    another operation x29 -> x14, other arithmetic: 149 us -> 78.8 us  [lower_inverse(): cholesky_low = jnp.linalg.cholesky(matrix)]
    reduce_scatter x1 -> x0, waiting for transfers between devices: 58 us -> none  [on_device(): lax.psum_scatter(lax.dot_general(factor, factor, (((0,), (0,)), ((), ()))...]
    another operation x8 -> x3, other arithmetic: 79.7 us -> 40.3 us  [lower_inverse(): return jax.scipy.linalg.solve_triangular(cholesky_low, identity, lower=True)]
    all_gather x1 -> x0, waiting for transfers between devices: 37.3 us -> none  [on_device(): gram_sum = lax.all_gather(gram_share, ('rows', 'sub'), axis=0, tiled=True)]
    another operation x16 -> x1, local copies, waits for them, and re-layouts: 8.21 us -> 0.01 us  [lower_inverse(): return jax.scipy.linalg.solve_triangular(cholesky_low, identity, lower=True)]
  transfers between devices with their start and end apart: 4 -> 2, of which waited for: 4 -> 2; matrix products, arithmetic and copies ran while one was open for 1% -> 0% of each run, Pallas kernels for 0% -> 0%
where the time goes in v1:
time: 356 us
  waiting for transfers between devices  188 us (53%)
  other arithmetic  123 us (35%)
  between operations  16.2 us (5%)
  matrix products  15.6 us (4%)
  local copies, waits for them, and re-layouts  12.8 us (4%)
    psum x1, waiting for transfers between devices, on_device(): piv_rows = lax.psum(mine, ('rows', 'sub'))  96.8 us
    psum x1, waiting for transfers between devices, on_device(): lax.psum(lax.dot_general(tile, tile, (((0,), (0,)), ((), ())), precision=...  91.6 us
    another operation x14, other arithmetic, lower_inverse(): cholesky_low = jnp.linalg.cholesky(matrix)  78.8 us
    another operation x3, other arithmetic, lower_inverse(): return jax.scipy.linalg.solve_triangular(cholesky_low, identity, lower=True)  40.3 us
    another operation x12, local copies, waits for them, and re-layouts  10.5 us
  transfers between devices with their start and end apart: 2, of which 2 were waited for; matrix products, arithmetic and copies ran while one was open for 0% of the time, Pallas kernels for 0%

profile of v1, /device:TPU:0, one launch (start us, length us, event | category | flops | bytes accessed | tf_op | source)
XLA Modules:
  0.0 355.8 jit_solution(12108948218079254002)
XLA Ops:
  6.5 0.7 subtract_bitcast_fusion
  7.2 2.6 convolution_convert_fusion
  10.1 96.8 %all-reduce.4.cloned.1.call-done = bf16[512,1024]{1,0:T(8,128)(2,1)} async-done(((bf16[512,1024]{1,0:T(8,128)(2,1)}), bf16[512,1024]{1,0:T(8,128)(2,1)}) %all-reduce.4.cloned.1.call-update) | async-done | bytes 1048592 | tf_op jit(solution)/shard_map/psum | solution.py:34
  106.9 1.6 multiply_reduce_fusion
  109.0 0.8 copy-done.3
  109.8 2.1 fusion.52
  111.9 0.8 iota_compare_fusion
  112.9 91.6 %all-reduce.6.cloned.1.call-done = f32[512,512]{0,1:T(8,128)} async-done(((f32[512,512]{0,1:T(8,128)}), f32[512,512]{0,1:T(8,128)}) %all-reduce.6.cloned.1.call-update) | async-done | bytes 1048592 | tf_op jit(solution)/shard_map/psum | solution.py:38
  204.5 2.1 fusion.5
  207.2 1.0 copy-done
  208.2 11.7 %cholesky.104 = f32[128,128]{1,0:T(8,128)S(1)} custom-call(f32[128,128]{1,0:T(8,128)S(1)} %cholesky.266), custom_call_target="Cholesky" | custom-call | tf_op jit(solution)/shard_map/jit(cholesky)/cholesky | solution.py:22
  220.0 9.8 %custom-call.31 = f32[1,128,128]{1,2,0:T(8,128)S(1)} custom-call(f32[1,128,128]{2,1,0:T(8,128)S(1)} %get-tuple-element.32), custom_call_target="InvertDiagBlocksLowerTriangular" | custom-call | tf_op jit(solution)/shard_map/jit(cholesky)/cholesky | solution.py:22
  230.6 11.9 %cholesky.217 = f32[128,128]{1,0:T(8,128)S(1)} custom-call(f32[128,128]{1,0:T(8,128)S(1)} %cholesky.270), custom_call_target="Cholesky" | custom-call | tf_op jit(solution)/shard_map/jit(cholesky)/cholesky | solution.py:22
  242.5 9.8 %custom-call.32 = f32[1,128,128]{1,2,0:T(8,128)S(1)} custom-call(f32[1,128,128]{2,1,0:T(8,128)S(1)} %get-tuple-element.29), custom_call_target="InvertDiagBlocksLowerTriangular" | custom-call | tf_op jit(solution)/shard_map/jit(cholesky)/cholesky | solution.py:22
  253.0 11.7 %cholesky.238 = f32[128,128]{1,0:T(8,128)S(1)} custom-call(f32[128,128]{1,0:T(8,128)S(1)} %cholesky.275), custom_call_target="Cholesky" | custom-call | tf_op jit(solution)/shard_map/jit(cholesky)/cholesky | solution.py:22
  264.7 0.7 compare_reduce_fusion.1
  265.5 9.8 %custom-call.33 = f32[1,128,128]{1,2,0:T(8,128)S(1)} custom-call(f32[1,128,128]{2,1,0:T(8,128)S(1)} %get-tuple-element.26), custom_call_target="InvertDiagBlocksLowerTriangular" | custom-call | tf_op jit(solution)/shard_map/jit(cholesky)/cholesky | solution.py:22
  275.9 11.9 %cholesky.255 = f32[128,128]{1,0:T(8,128)S(1)} custom-call(f32[128,128]{1,0:T(8,128)S(1)} %convolution_subtract_fusion.5), custom_call_target="Cholesky" | custom-call | tf_op jit(solution)/shard_map/jit(cholesky)/cholesky | solution.py:22
  287.8 0.6 compare_reduce_fusion
  288.4 0.7 compare_reduce_fusion.2
  291.8 10.6 %while.1 = (s32[]{:T(128)}, f32[512,512]{1,0:T(8,128)S(1)}, s32[4,2]{0,1:T(2,128)S(1)}, f32[4,128,128]{2,1,0:T(8,128)}, s32[]{:T(128)}) while((s32[]{:T(128)}, f32[512,512]{1,0:T(8,128)S(1)}, s32[4,2]{0,1:T(2,128)S(1)}, f32[4,128,128]{2,1,0:T(8,128)}, s32[]{:T(128)}) %tuple.27), condition=%wide.while_cond, body=%wide.while_body.sunk | while | flops 2 | bytes 132705 | solution.py:24
  291.9 0.6 fusion.67
  292.5 2.0 bitcast_dynamic-update-slice_fusion.2
  294.5 0.6 fusion.67
  295.1 2.0 bitcast_dynamic-update-slice_fusion.2
  297.2 0.6 fusion.67
  297.8 2.0 bitcast_dynamic-update-slice_fusion.2
  300.4 2.0 bitcast_dynamic-update-slice_fusion.2
  302.4 40.1 %custom-call.34 = f32[4,128,128]{1,2,0:T(8,128)S(1)} custom-call(f32[4,128,128]{2,1,0:T(8,128)} %get-tuple-element.12), custom_call_target="InvertDiagBlocksLowerTriangular" | custom-call | tf_op jit(solution)/shard_map/jit(_solve_triangular)/triangular_solve | solution.py:24
  342.5 1.1 fusion.30
  345.3 0.6 convolution_subtract_fusion.2
  346.3 2.7 fusion.10
  (48 shorter events, 6.7 us)
Async XLA Ops:
  6.5 100.4 %all-reduce.4.cloned.1.call-start = ((), (), s32[]{:S(2)}) async-start(), calls=%async_computation | async-start | bytes 2097152 | tf_op jit(solution)/shard_map/psum | solution.py:34
  7.2 2.7 copy-start.2
  9.9 194.6 %all-reduce.6.cloned.1.call-start = ((), (), s32[]{:S(2)}) async-start(), calls=%async_computation.1 | async-start | bytes 2097152 | tf_op jit(solution)/shard_map/psum | solution.py:38
  106.9 1.6 copy-start.5
  109.0 0.8 copy-start.3
  207.2 1.0 copy-start
  208.2 21.7 %copy-start.1 = (f32[512,512]{1,0:T(8,128)S(1)}, f32[512,512]{1,0:T(8,128)}, u32[]{:S(2)}) copy-start(f32[512,512]{1,0:T(8,128)} %copy-done) | copy-start | bytes 3145732
  345.2 1.1 copy-start.4
Sparse Core Ops, SparseCore 0:
  10.8 96.0 all-reduce.3
  112.0 92.3 all-reduce.5

commit v2 on v1

v2 whole, which is shorter than its diff:
```python
import functools

import jax
import jax.numpy as jnp
from jax import lax
from jax.experimental import pallas as pl
from jax.experimental.pallas import tpu as pltpu
from jax.sharding import PartitionSpec as P

ridge_shift = 0.001
EXACT = lax.Precision.HIGHEST
GROUP = 16
TILE = 128


def squares(points):
    return jnp.sum(jnp.square(points.astype(jnp.float32)), axis=1)


def kernel_tile(points, point_sq, others, other_sq):
    products = lax.dot_general(
        points, others, (((1,), (1,)), ((), ())), preferred_element_type=jnp.float32
    )
    return jnp.exp((2.0 * products - point_sq[:, None] - other_sq[None, :]) / points.shape[1])


def exact_dot(first, second, first_dim, second_dim):
    return lax.dot_general(
        first,
        second,
        (((first_dim,), (second_dim,)), ((), ())),
        precision=EXACT,
        preferred_element_type=jnp.float32,
    )


def tile_inverse(tile):
    lane = lax.broadcasted_iota(jnp.int32, (GROUP, TILE), 1)
    sub = lax.broadcasted_iota(jnp.int32, (GROUP, TILE), 0)
    count = TILE // GROUP
    groups = [tile[g * GROUP:(g + 1) * GROUP] for g in range(count)]
    wide = functools.partial(jnp.broadcast_to, shape=(GROUP, TILE))
    for g in range(count):
        start = g * GROUP
        rows = groups[g]
        cols = [wide(rows[:, start + j:start + j + 1]) for j in range(GROUP)]
        for j in range(GROUP):
            scale = lax.rsqrt(wide(cols[j][j:j + 1]))
            below = jnp.where(sub > j, cols[j] * scale, 0.0)
            for k in range(j + 1, GROUP):
                cols[k] = cols[k] - below * (wide(cols[k][j:j + 1]) * scale)
            row = jnp.where(lane == start + j, scale, wide(rows[j:j + 1]) * scale)
            rest = jnp.where((lane == start + j) & (sub > j), 0.0, rows)
            rows = jnp.where(sub == j, row, rest - below * row)
        rows = jnp.where((lane > start + sub) & (lane < start + GROUP), 0.0, rows)
        groups[g] = rows
        if g + 1 < count:
            change = exact_dot(rows, rows, 0, 0)
            inside = (lane >= start) & (lane < start + GROUP)
            for h in range(g + 1, count):
                groups[h] = jnp.where(inside, 0.0, groups[h]) - change[h * GROUP:(h + 1) * GROUP]
    whole = jnp.concatenate(groups, axis=0)
    row_id = lax.broadcasted_iota(jnp.int32, (TILE, TILE), 0)
    lane_id = lax.broadcasted_iota(jnp.int32, (TILE, TILE), 1)
    return jnp.where(lane_id <= row_id, whole, 0.0)


def inverse_kernel(a_ref, w_ref, work):
    size = a_ref.shape[0]
    work[...] = a_ref[...]
    row_block = lax.broadcasted_iota(jnp.int32, (size, size), 0) // TILE
    col_block = lax.broadcasted_iota(jnp.int32, (size, size), 1) // TILE
    panel_block = lax.broadcasted_iota(jnp.int32, (TILE, size), 1) // TILE

    def step(block, carry):
        start = pl.multiple_of(block * TILE, TILE)
        here = pl.ds(start, TILE)
        small = tile_inverse(work[here, here])
        work[here, :] = exact_dot(small, work[here, :], 1, 0)
        work[here, here] = small
        panel = work[here, :]
        change = exact_dot(jnp.where(panel_block > block, panel, 0.0), panel, 0, 0)
        fresh = (row_block > block) & (col_block == block)
        work[...] = jnp.where(fresh, 0.0, work[...]) - change
        return carry

    lax.fori_loop(0, size // TILE, step, 0)
    row_id = lax.broadcasted_iota(jnp.int32, (size, size), 0)
    col_id = lax.broadcasted_iota(jnp.int32, (size, size), 1)
    w_ref[...] = jnp.where(col_id <= row_id, work[...], 0.0)


def lower_inverse(matrix):
    return pl.pallas_call(
        inverse_kernel,
        out_shape=jax.ShapeDtypeStruct(matrix.shape, jnp.float32),
        in_specs=[pl.BlockSpec(memory_space=pltpu.VMEM)],
        out_specs=pl.BlockSpec(memory_space=pltpu.VMEM),
        scratch_shapes=[pltpu.VMEM(matrix.shape, jnp.float32)],
        compiler_params=pltpu.CompilerParams(vmem_limit_bytes=32 * 2**20),
        name="lower_inverse",
    )(matrix)


def sum_kernel(in_ref, out_ref, half, quarter, parts, total, send, recv):
    pieces, rows, width = in_ref.shape
    z = lax.axis_index("rows")
    spot = lax.axis_index("sub")
    x, core = spot // 2, spot % 2
    peers = [{"sub": x * 2 + 1 - core}, {"sub": (1 - x) * 2 + core}]
    peers += [{"rows": (z + o) % 4} for o in (1, 2, 3)]
    barrier = pltpu.get_barrier_semaphore()
    for peer in peers:
        pl.semaphore_signal(barrier, inc=1, device_id=peer, device_id_type=pl.DeviceIdType.MESH)
    pl.semaphore_wait(barrier, len(peers))

    n2, n4, n16 = rows // 2, rows // 4, rows // 16

    def cut(start, size):
        return pl.ds(pl.multiple_of(start, n16), size)

    half_at = core * n2
    quarter_at = half_at + x * n4
    mine_at = quarter_at + z * n16

    def move(p, slot, src, dst, peer):
        return pltpu.make_async_remote_copy(
            src_ref=src, dst_ref=dst, send_sem=send.at[p, slot], recv_sem=recv.at[p, slot],
            device_id=peers[peer], device_id_type=pl.DeviceIdType.MESH,
        )

    first, second, third, fourth, fifth, sixth = [], [], [], [], [], []
    for p in range(pieces):
        copy = move(p, 0, in_ref.at[p, cut((1 - core) * n2, n2)], half.at[p], 0)
        copy.start()
        first.append(copy)
    for p in range(pieces):
        first[p].wait_recv()
        half[p] = half[p] + in_ref[p, cut(half_at, n2)]
        copy = move(p, 1, half.at[p, cut((1 - x) * n4, n4)], quarter.at[p], 1)
        copy.start()
        second.append(copy)
    for p in range(pieces):
        second[p].wait_recv()
        quarter[p] = quarter[p] + half[p, cut(x * n4, n4)]
        copies = []
        for o in (1, 2, 3):
            copy = move(p, 1 + o, quarter.at[p, cut(((z + o) % 4) * n16, n16)], parts.at[p, o - 1], 1 + o)
            copy.start()
            copies.append(copy)
        third.append(copies)
    for p in range(pieces):
        value = quarter[p, cut(z * n16, n16)]
        for o in (1, 2, 3):
            third[p][o - 1].wait_recv()
            value = value + parts[p, o - 1]
        total[p, cut(mine_at, n16)] = value
        copies = []
        for o in (1, 2, 3):
            place = total.at[p, cut(mine_at, n16)]
            copy = move(p, 4 + o, place, place, 1 + o)
            copy.start()
            copies.append(copy)
        fourth.append(copies)
    for p in range(pieces):
        for copy in fourth[p]:
            copy.wait_recv()
        place = total.at[p, cut(quarter_at, n4)]
        copy = move(p, 8, place, place, 1)
        copy.start()
        fifth.append(copy)
    for p in range(pieces):
        fifth[p].wait_recv()
        place = total.at[p, cut(half_at, n2)]
        copy = move(p, 9, place, place, 0)
        copy.start()
        sixth.append(copy)
    for p in range(pieces):
        sixth[p].wait_recv()
        out_ref[p] = total[p]
    for p in range(pieces):
        for copy in [first[p], second[p], *third[p], *fourth[p], fifth[p], sixth[p]]:
            copy.wait_send()


def group_sum(array, collective_id):
    if lax.axis_size("rows") != 4 or lax.axis_size("sub") != 4:
        return lax.psum(array, ("rows", "sub"))
    pieces, rows, width = array.shape
    kind = array.dtype
    return pl.pallas_call(
        sum_kernel,
        out_shape=jax.ShapeDtypeStruct(array.shape, kind),
        in_specs=[pl.BlockSpec(memory_space=pltpu.VMEM)],
        out_specs=pl.BlockSpec(memory_space=pltpu.VMEM),
        scratch_shapes=[
            pltpu.VMEM((pieces, rows // 2, width), kind),
            pltpu.VMEM((pieces, rows // 4, width), kind),
            pltpu.VMEM((pieces, 3, rows // 16, width), kind),
            pltpu.VMEM(array.shape, kind),
            pltpu.SemaphoreType.DMA((pieces, 10)),
            pltpu.SemaphoreType.DMA((pieces, 10)),
        ],
        compiler_params=pltpu.CompilerParams(
            collective_id=collective_id, has_side_effects=True, vmem_limit_bytes=32 * 2**20
        ),
        name="group_sum_" + str(collective_id),
    )(array)


def on_device(embeddings, pivots):
    local_count, width = embeddings.shape
    devices = lax.axis_size(("rows", "sub"))
    first_row = lax.axis_index(("rows", "sub")) * local_count
    spots = pivots.reshape(-1) - first_row
    count = spots.shape[0]
    chosen = (spots[:, None] == lax.iota(jnp.int32, local_count)[None, :]).astype(jnp.bfloat16)
    pieces = 4
    step = width // pieces
    mine = jnp.stack([
        jnp.dot(chosen, embeddings[:, p * step:(p + 1) * step], preferred_element_type=jnp.float32)
        .astype(jnp.bfloat16) for p in range(pieces)
    ])
    got = group_sum(mine, 0)
    piv_rows = jnp.concatenate([got[p] for p in range(pieces)], axis=1)
    norms = squares(embeddings)
    piv_sq = squares(piv_rows)
    tile = kernel_tile(embeddings, norms, piv_rows, piv_sq)
    pivot_gram = kernel_tile(piv_rows, piv_sq, piv_rows, piv_sq)
    factor = exact_dot(tile, lower_inverse(pivot_gram), 1, 1)
    share = exact_dot(factor, factor, 0, 0)
    low = count // 2
    packed = jnp.stack([share[:low, :low], share[low:, :low], share[low:, low:]])
    packed = group_sum(packed, 1) / (local_count * devices)
    gram = jnp.block([[packed[0], packed[1].T], [packed[1], packed[2]]])
    gram = gram + ridge_shift * jnp.eye(count, dtype=jnp.float32)
    return exact_dot(factor, lower_inverse(gram), 1, 1)


def solution(mesh):
    return jax.shard_map(
        on_device,
        mesh=mesh,
        in_specs=(P(("groups", "rows", "sub"), None), P("groups", None)),
        out_specs=P(("groups", "rows", "sub"), None),
        check_vma=False,
    )
```

time: 356 us -> 112 us (0.31)
  waiting for transfers between devices: 188 us -> 0 us
  other arithmetic: 123 us -> 2.66 us
  Pallas kernels: 0 us -> 99.4 us
  between operations: 16.2 us -> 0.16 us
  local copies, waits for them, and re-layouts: 12.8 us -> 0.55 us
  matrix products: 15.6 us -> 8.98 us
    psum x2 -> x0, waiting for transfers between devices: 188 us -> none  [the longest x1 96.8 us: on_device(): piv_rows = lax.psum(mine, ('rows', 'sub'))]
    another operation x17 -> x2, other arithmetic: 119 us -> 0.19 us  [the longest x1 0.14 us: on_device(): jnp.stack([jnp.dot(chosen, embeddings[:, p * step:(p + 1) * step], prefer...]
    pallas_call x0 -> x4, Pallas kernels: none -> 99.4 us  [the longest x2 52.3 us: group_sum(): pl.pallas_call(sum_kernel, out_shape=jax.ShapeDtypeStruct(array.shape, ki...]
    another operation x17 -> x1, local copies, waits for them, and re-layouts: 10.7 us -> 0.06 us  [on_device(): jnp.stack([share[:low, :low], share[low:, :low], share[low:, low:]])]
    another operation x13 -> x0, matrix products: 5.64 us -> none  [the longest x7 3.77 us: lower_inverse(): return jax.scipy.linalg.solve_triangular(cholesky_low, identity, lower=True)]
    dot_general x3 -> x7, matrix products: 7.38 us -> 7.68 us  [the longest x3 4.76 us: exact_dot(): lax.dot_general(first, second, (((first_dim,), (second_dim,)), ((), ())),...]
  transfers between devices with their start and end apart: 2 -> 0, of which waited for: 2 -> 0; matrix products, arithmetic and copies ran while one was open for 0% -> 0% of each run, Pallas kernels for 0% -> 0%
where the time goes in v2:
time: 112 us
  Pallas kernels  99.4 us (89%)
  matrix products  8.98 us (8%)
  other arithmetic  2.66 us (2%)
    pallas_call x2, Pallas kernels, group_sum(): pl.pallas_call(sum_kernel, out_shape=jax.ShapeDtypeStruct(array.shape, ki...  52.3 us
    pallas_call x2, Pallas kernels, lower_inverse(): pl.pallas_call(inverse_kernel, out_shape=jax.ShapeDtypeStruct(matrix.shap...  47.2 us
    dot_general x3, matrix products, exact_dot(): lax.dot_general(first, second, (((first_dim,), (second_dim,)), ((), ())),...  4.76 us
    dot_general x4, matrix products, on_device(): jnp.dot(chosen, embeddings[:, p * step:(p + 1) * step], preferred_element...  2.92 us

profile of v2, /device:TPU:0, one launch (start us, length us, event | category | flops | bytes accessed | tf_op | source)
XLA Modules:
  0.0 111.8 jit_solution(8370751536130969521)
XLA Ops:
  0.0 0.0 copy-start
  0.0 1.3 %multiply_reduce_fusion.1 = f32[256]{0:T(256)S(1)} fusion(bf16[256,1024]{1,0:T(8,128)(2,1)} %param.2), kind=kLoop, calls=%fused_computation.23 | loop fusion | flops 786176 | bytes 525312 | tf_op jit(solution)/shard_map/reduce_sum | solution.py:17
  1.3 0.7 subtract_bitcast_fusion
  2.0 1.2 %fusion.11 = bf16[1,512,256]{2,1,0:T(8,128)(2,1)S(1)} fusion(s32[512]{0:T(512)S(1)} %bitcast.41, bf16[256,1024]{1,0:T(8,128)(2,1)} %param.2), kind=kOutput, calls=%fused_computation.18 | convolution fusion | flops 67371008 | bytes 395264 | tf_op jit(solution)/shard_map/dot_general | solution.py:221
  3.2 1.2 %fusion.10 = bf16[1,512,256]{2,1,0:T(8,128)(2,1)S(1)} fusion(s32[512]{0:T(512)S(1)} %bitcast.42, bf16[256,1024]{1,0:T(8,128)(2,1)} %param.2), kind=kOutput, calls=%fused_computation.17 | convolution fusion | flops 67371008 | bytes 395264 | tf_op jit(solution)/shard_map/dot_general | solution.py:221
  4.4 0.0 copy-done
  4.4 0.3 fusion.9
  4.6 0.3 fusion.8
  4.9 0.1 pad_maximum_fusion.in_ref
  5.1 27.8 %group_sum_0.1 = bf16[4,512,256]{2,1,0:T(8,128)(2,1)S(1)} custom-call(bf16[4,512,256]{2,1,0:T(8,128)(2,1)S(1)} %pad_maximum_fusion.in_ref), custom_call_target="tpu_custom_call" | custom-call | tf_op jit(solution)/shard_map/group_sum_0/pallas_call | solution.py:191
  32.9 0.1 slice_bitcast_fusion.7
  32.9 0.3 multiply_reduce_fusion
  33.2 0.5 fusion.7
  33.7 0.8 fusion.3.a_ref
  34.5 23.7 %lower_inverse.2 = f32[512,512]{1,0:T(8,128)S(1)} custom-call(f32[512,512]{1,0:T(8,128)S(1)} %fusion.3.a_ref), custom_call_target="tpu_custom_call" | custom-call | tf_op jit(solution)/shard_map/lower_inverse/pallas_call | solution.py:94
  58.2 1.9 %fusion.21 = f32[256,512]{1,0:T(8,128)S(1)} fusion(f32[512,256]{1,0:T(8,128)S(1)} %fusion.7, f32[512,512]{1,0:T(8,128)S(1)} %lower_inverse.2), kind=kOutput, calls=%fused_computation.48 | convolution fusion | flops 805306368 | bytes 2097152 | tf_op jit(solution)/shard_map/dot_general | solution.py:28
  60.1 1.0 fusion.22
  61.1 0.1 slice_bitcast_fusion.3
  61.2 0.1 pad_maximum_fusion.2.in_ref
  61.3 24.5 %group_sum_1.1 = f32[3,256,256]{2,1,0:T(8,128)S(1)} custom-call(f32[3,256,256]{2,1,0:T(8,128)S(1)} %pad_maximum_fusion.2.in_ref), custom_call_target="tpu_custom_call" | custom-call | tf_op jit(solution)/shard_map/group_sum_1/pallas_call | solution.py:191
  85.8 0.1 broadcast_multiply_fusion
  85.8 0.1 fusion.20
  85.9 0.1 copy.5
  86.1 0.2 copy.4
  86.3 0.1 maximum_add_fusion.a_ref
  86.4 23.5 %lower_inverse.3 = f32[512,512]{1,0:T(8,128)S(1)} custom-call(f32[512,512]{1,0:T(8,128)S(1)} %maximum_add_fusion.a_ref), custom_call_target="tpu_custom_call" | custom-call | tf_op jit(solution)/shard_map/lower_inverse/pallas_call | solution.py:94
  109.9 1.9 %fusion.23 = f32[256,512]{1,0:T(8,128)} fusion(f32[256,512]{1,0:T(8,128)S(1)} %fusion.21, f32[512,512]{1,0:T(8,128)S(1)} %lower_inverse.3), kind=kOutput, calls=%fused_computation.50 | convolution fusion | flops 805306368 | bytes 2097152 | tf_op jit(solution)/shard_map/dot_general | solution.py:28
  (2 shorter events, 0.0 us)
Async XLA Ops:
  0.0 4.4 %copy-start = (bf16[256,1024]{1,0:T(8,128)(2,1)S(1)}, bf16[256,1024]{1,0:T(8,128)(2,1)}, u32[]{:S(2)}) copy-start(bf16[256,1024]{1,0:T(8,128)(2,1)} %param.2) | copy-start | bytes 1572868

commit v3 on v2

--- a/solution.py
+++ b/solution.py
@@ -42,52 +42,58 @@
     wide = functools.partial(jnp.broadcast_to, shape=(GROUP, TILE))
     for g in range(count):
         start = g * GROUP
+        end = start + GROUP
         rows = groups[g]
         cols = [wide(rows[:, start + j:start + j + 1]) for j in range(GROUP)]
         for j in range(GROUP):
             scale = lax.rsqrt(wide(cols[j][j:j + 1]))
+            over = scale * scale
+            for k in range(j + 1, GROUP):
+                cols[k] = cols[k] - (cols[j] * wide(cols[k][j:j + 1])) * over
             below = jnp.where(sub > j, cols[j] * scale, 0.0)
-            for k in range(j + 1, GROUP):
-                cols[k] = cols[k] - below * (wide(cols[k][j:j + 1]) * scale)
             row = jnp.where(lane == start + j, scale, wide(rows[j:j + 1]) * scale)
             rest = jnp.where((lane == start + j) & (sub > j), 0.0, rows)
             rows = jnp.where(sub == j, row, rest - below * row)
-        rows = jnp.where((lane > start + sub) & (lane < start + GROUP), 0.0, rows)
+        rows = jnp.where((lane > start + sub) & (lane < end), 0.0, rows)
         groups[g] = rows
+        inside = (lane >= start) & (lane < end)
         if g + 1 < count:
-            change = exact_dot(rows, rows, 0, 0)
-            inside = (lane >= start) & (lane < start + GROUP)
-            for h in range(g + 1, count):
-                groups[h] = jnp.where(inside, 0.0, groups[h]) - change[h * GROUP:(h + 1) * GROUP]
+            change = exact_dot(rows[:, end:end + GROUP], rows, 0, 0)
+            groups[g + 1] = jnp.where(inside, 0.0, groups[g + 1]) - change
+        if g + 2 < count:
+            change = exact_dot(rows[:, end + GROUP:], rows, 0, 0)
+            for h in range(g + 2, count):
+                at = (h - g - 2) * GROUP
+                groups[h] = jnp.where(inside, 0.0, groups[h]) - change[at:at + GROUP]
     whole = jnp.concatenate(groups, axis=0)
     row_id = lax.broadcasted_iota(jnp.int32, (TILE, TILE), 0)
     lane_id = lax.broadcasted_iota(jnp.int32, (TILE, TILE), 1)
     return jnp.where(lane_id <= row_id, whole, 0.0)
 
 
-def inverse_kernel(a_ref, w_ref, work):
+def inverse_kernel(a_ref, w_ref, upper):
     size = a_ref.shape[0]
-    work[...] = a_ref[...]
-    row_block = lax.broadcasted_iota(jnp.int32, (size, size), 0) // TILE
-    col_block = lax.broadcasted_iota(jnp.int32, (size, size), 1) // TILE
-    panel_block = lax.broadcasted_iota(jnp.int32, (TILE, size), 1) // TILE
-
-    def step(block, carry):
-        start = pl.multiple_of(block * TILE, TILE)
-        here = pl.ds(start, TILE)
-        small = tile_inverse(work[here, here])
-        work[here, :] = exact_dot(small, work[here, :], 1, 0)
-        work[here, here] = small
-        panel = work[here, :]
-        change = exact_dot(jnp.where(panel_block > block, panel, 0.0), panel, 0, 0)
-        fresh = (row_block > block) & (col_block == block)
-        work[...] = jnp.where(fresh, 0.0, work[...]) - change
-        return carry
-
-    lax.fori_loop(0, size // TILE, step, 0)
-    row_id = lax.broadcasted_iota(jnp.int32, (size, size), 0)
-    col_id = lax.broadcasted_iota(jnp.int32, (size, size), 1)
-    w_ref[...] = jnp.where(col_id <= row_id, work[...], 0.0)
+    count = size // TILE
+    w_ref[...] = jnp.zeros_like(w_ref)
+
+    def at(block):
+        return slice(block * TILE, (block + 1) * TILE)
+
+    for j in range(count):
+        square = a_ref[at(j), at(j)]
+        for k in range(j):
+            square = square - exact_dot(upper[at(k), at(j)], upper[at(k), at(j)], 0, 0)
+        small = tile_inverse(square)
+        for i in range(j + 1, count):
+            block = a_ref[at(j), at(i)]
+            for k in range(j):
+                block = block - exact_dot(upper[at(k), at(j)], upper[at(k), at(i)], 0, 0)
+            upper[at(j), at(i)] = exact_dot(small, block, 1, 0)
+        w_ref[at(j), at(j)] = small
+        if j:
+            known = slice(0, j * TILE)
+            left = exact_dot(upper[known, at(j)], w_ref[known, known], 0, 0)
+            w_ref[at(j), known] = -exact_dot(small, left, 1, 0)
 
 
 def lower_inverse(matrix):

time: 112 us -> 104 us (0.929)
  Pallas kernels: 99.4 us -> 91.7 us
    pallas_call x2, Pallas kernels: 47.2 us -> 39.4 us  [lower_inverse(): pl.pallas_call(inverse_kernel, out_shape=jax.ShapeDtypeStruct(matrix.shap...]
where the time goes in v3:
time: 104 us
  Pallas kernels  91.7 us (88%)
  matrix products  8.99 us (9%)
  other arithmetic  2.66 us (3%)
    pallas_call x2, Pallas kernels, group_sum(): pl.pallas_call(sum_kernel, out_shape=jax.ShapeDtypeStruct(array.shape, ki...  52.2 us
    pallas_call x2, Pallas kernels, lower_inverse(): pl.pallas_call(inverse_kernel, out_shape=jax.ShapeDtypeStruct(matrix.shap...  39.4 us
    dot_general x3, matrix products, exact_dot(): lax.dot_general(first, second, (((first_dim,), (second_dim,)), ((), ())),...  4.76 us
    dot_general x4, matrix products, on_device(): jnp.dot(chosen, embeddings[:, p * step:(p + 1) * step], preferred_element...  2.92 us

profile of v3, /device:TPU:0, one launch (start us, length us, event | category | flops | bytes accessed | tf_op | source)
XLA Modules:
  0.0 104.0 jit_solution(4648143779014709073)
XLA Ops:
  0.0 0.0 copy-start
  0.0 1.3 %multiply_reduce_fusion.1 = f32[256]{0:T(256)S(1)} fusion(bf16[256,1024]{1,0:T(8,128)(2,1)} %param.2), kind=kLoop, calls=%fused_computation.23 | loop fusion | flops 786176 | bytes 525312 | tf_op jit(solution)/shard_map/reduce_sum | solution.py:17
  1.3 0.7 subtract_bitcast_fusion
  2.0 1.2 %fusion.11 = bf16[1,512,256]{2,1,0:T(8,128)(2,1)S(1)} fusion(s32[512]{0:T(512)S(1)} %bitcast.41, bf16[256,1024]{1,0:T(8,128)(2,1)} %param.2), kind=kOutput, calls=%fused_computation.18 | convolution fusion | flops 67371008 | bytes 395264 | tf_op jit(solution)/shard_map/dot_general | solution.py:227
  3.2 1.2 %fusion.10 = bf16[1,512,256]{2,1,0:T(8,128)(2,1)S(1)} fusion(s32[512]{0:T(512)S(1)} %bitcast.42, bf16[256,1024]{1,0:T(8,128)(2,1)} %param.2), kind=kOutput, calls=%fused_computation.17 | convolution fusion | flops 67371008 | bytes 395264 | tf_op jit(solution)/shard_map/dot_general | solution.py:227
  4.4 0.0 copy-done
  4.4 0.3 fusion.9
  4.6 0.3 fusion.8
  4.9 0.1 pad_maximum_fusion.in_ref
  5.1 27.8 %group_sum_0.1 = bf16[4,512,256]{2,1,0:T(8,128)(2,1)S(1)} custom-call(bf16[4,512,256]{2,1,0:T(8,128)(2,1)S(1)} %pad_maximum_fusion.in_ref), custom_call_target="tpu_custom_call" | custom-call | tf_op jit(solution)/shard_map/group_sum_0/pallas_call | solution.py:197
  32.9 0.1 slice_bitcast_fusion.7
  32.9 0.3 multiply_reduce_fusion
  33.2 0.5 fusion.7
  33.7 0.8 fusion.3.a_ref
  34.5 19.7 %lower_inverse.2 = f32[512,512]{1,0:T(8,128)S(1)} custom-call(f32[512,512]{1,0:T(8,128)S(1)} %fusion.3.a_ref), custom_call_target="tpu_custom_call" | custom-call | tf_op jit(solution)/shard_map/lower_inverse/pallas_call | solution.py:100
  54.3 1.9 %fusion.21 = f32[256,512]{1,0:T(8,128)S(1)} fusion(f32[512,256]{1,0:T(8,128)S(1)} %fusion.7, f32[512,512]{1,0:T(8,128)S(1)} %lower_inverse.2), kind=kOutput, calls=%fused_computation.48 | convolution fusion | flops 805306368 | bytes 2097152 | tf_op jit(solution)/shard_map/dot_general | solution.py:28
  56.1 1.0 %fusion.22 = f32[512,512]{1,0:T(8,128)S(1)} fusion(f32[256,512]{1,0:T(8,128)S(1)} %fusion.21), kind=kOutput, calls=%fused_computation.49 | convolution fusion | flops 805306368 | bytes 1572864 | tf_op jit(solution)/shard_map/dot_general | solution.py:28
  57.2 0.1 slice_bitcast_fusion.3
  57.2 0.1 pad_maximum_fusion.2.in_ref
  57.3 24.5 %group_sum_1.1 = f32[3,256,256]{2,1,0:T(8,128)S(1)} custom-call(f32[3,256,256]{2,1,0:T(8,128)S(1)} %pad_maximum_fusion.2.in_ref), custom_call_target="tpu_custom_call" | custom-call | tf_op jit(solution)/shard_map/group_sum_1/pallas_call | solution.py:197
  81.8 0.1 broadcast_multiply_fusion
  81.8 0.1 fusion.20
  81.9 0.1 copy.5
  82.1 0.2 copy.4
  82.3 0.1 maximum_add_fusion.a_ref
  82.4 19.7 %lower_inverse.3 = f32[512,512]{1,0:T(8,128)S(1)} custom-call(f32[512,512]{1,0:T(8,128)S(1)} %maximum_add_fusion.a_ref), custom_call_target="tpu_custom_call" | custom-call | tf_op jit(solution)/shard_map/lower_inverse/pallas_call | solution.py:100
  102.2 1.9 %fusion.23 = f32[256,512]{1,0:T(8,128)} fusion(f32[256,512]{1,0:T(8,128)S(1)} %fusion.21, f32[512,512]{1,0:T(8,128)S(1)} %lower_inverse.3), kind=kOutput, calls=%fused_computation.50 | convolution fusion | flops 805306368 | bytes 2097152 | tf_op jit(solution)/shard_map/dot_general | solution.py:28
  (2 shorter events, 0.0 us)
Async XLA Ops:
  0.0 4.4 %copy-start = (bf16[256,1024]{1,0:T(8,128)(2,1)S(1)}, bf16[256,1024]{1,0:T(8,128)(2,1)}, u32[]{:S(2)}) copy-start(bf16[256,1024]{1,0:T(8,128)(2,1)} %param.2) | copy-start | bytes 1572868

commit v4 on v3

--- a/solution.py
+++ b/solution.py
@@ -11,6 +11,7 @@
 EXACT = lax.Precision.HIGHEST
 GROUP = 16
 TILE = 128
+PIECES = 4
 
 
 def squares(points):
@@ -108,7 +109,26 @@
     )(matrix)
 
 
-def sum_kernel(in_ref, out_ref, half, quarter, parts, total, send, recv):
+def pick_rows(spots_ref, points_ref, mine, piece):
+    local_count = points_ref.shape[0]
+    width = mine.shape[2]
+    lane = lax.broadcasted_iota(jnp.int32, (spots_ref.shape[0], local_count), 1)
+    chosen = jnp.where(spots_ref[...] == lane, 1.0, 0.0).astype(jnp.bfloat16)
+    block = points_ref[:, piece * width:(piece + 1) * width]
+    rows = jnp.dot(chosen, block, preferred_element_type=jnp.float32)
+    mine[piece] = rows.astype(mine.dtype)
+
+
+def pivot_kernel(spots_ref, points_ref, out_ref, norm_ref, mine, *scratch):
+    def beside():
+        values = points_ref[...].astype(jnp.float32)
+        norm_ref[...] = jnp.sum(values * values, axis=1, keepdims=True)
+
+    pick = functools.partial(pick_rows, spots_ref, points_ref, mine)
+    sum_kernel(mine, out_ref, *scratch, before=pick, beside=beside)
+
+
+def sum_kernel(in_ref, out_ref, half, quarter, parts, total, send, recv, before=None, beside=None):
     pieces, rows, width = in_ref.shape
     z = lax.axis_index("rows")
     spot = lax.axis_index("sub")
@@ -118,6 +138,8 @@
     barrier = pltpu.get_barrier_semaphore()
     for peer in peers:
         pl.semaphore_signal(barrier, inc=1, device_id=peer, device_id_type=pl.DeviceIdType.MESH)
+    if before:
+        before(0)
     pl.semaphore_wait(barrier, len(peers))
 
     n2, n4, n16 = rows // 2, rows // 4, rows // 16
@@ -137,6 +159,8 @@
 
     first, second, third, fourth, fifth, sixth = [], [], [], [], [], []
     for p in range(pieces):
+        if before and p:
+            before(p)
         copy = move(p, 0, in_ref.at[p, cut((1 - core) * n2, n2)], half.at[p], 0)
         copy.start()
         first.append(copy)
@@ -155,6 +179,8 @@
             copy.start()
             copies.append(copy)
         third.append(copies)
+    if beside:
+        beside()
     for p in range(pieces):
         value = quarter[p, cut(z * n16, n16)]
         for o in (1, 2, 3):
@@ -189,29 +215,63 @@
             copy.wait_send()
 
 
+def sum_scratch(shape, kind):
+    pieces, rows, width = shape
+    return [
+        pltpu.VMEM((pieces, rows // 2, width), kind),
+        pltpu.VMEM((pieces, rows // 4, width), kind),
+        pltpu.VMEM((pieces, 3, rows // 16, width), kind),
+        pltpu.VMEM(shape, kind),
+        pltpu.SemaphoreType.DMA((pieces, 10)),
+        pltpu.SemaphoreType.DMA((pieces, 10)),
+    ]
+
+
+def sum_params(collective_id):
+    return pltpu.CompilerParams(
+        collective_id=collective_id, has_side_effects=True, vmem_limit_bytes=32 * 2**20
+    )
+
+
+def sixteen():
+    return lax.axis_size("rows") == 4 and lax.axis_size("sub") == 4
+
+
 def group_sum(array, collective_id):
-    if lax.axis_size("rows") != 4 or lax.axis_size("sub") != 4:
+    if not sixteen():
         return lax.psum(array, ("rows", "sub"))
-    pieces, rows, width = array.shape
-    kind = array.dtype
     return pl.pallas_call(
         sum_kernel,
-        out_shape=jax.ShapeDtypeStruct(array.shape, kind),
+        out_shape=jax.ShapeDtypeStruct(array.shape, array.dtype),
         in_specs=[pl.BlockSpec(memory_space=pltpu.VMEM)],
         out_specs=pl.BlockSpec(memory_space=pltpu.VMEM),
-        scratch_shapes=[
-            pltpu.VMEM((pieces, rows // 2, width), kind),
-            pltpu.VMEM((pieces, rows // 4, width), kind),
-            pltpu.VMEM((pieces, 3, rows // 16, width), kind),
-            pltpu.VMEM(array.shape, kind),
-            pltpu.SemaphoreType.DMA((pieces, 10)),
-            pltpu.SemaphoreType.DMA((pieces, 10)),
-        ],
-        compiler_params=pltpu.CompilerParams(
-            collective_id=collective_id, has_side_effects=True, vmem_limit_bytes=32 * 2**20
-        ),
+        scratch_shapes=sum_scratch(array.shape, array.dtype),
+        compiler_params=sum_params(collective_id),
         name="group_sum_" + str(collective_id),
     )(array)
+
+
+def gather_pivots(spots, points, collective_id):
+    local_count, width = points.shape
+    count = spots.shape[0]
+    if not sixteen():
+        chosen = (spots[:, None] == lax.iota(jnp.int32, local_count)[None, :]).astype(points.dtype)
+        mine = jnp.dot(chosen, points, preferred_element_type=jnp.float32).astype(points.dtype)
+        return lax.psum(mine, ("rows", "sub")), squares(points)
+    shape = (PIECES, count, width // PIECES)
+    got, norms = pl.pallas_call(
+        pivot_kernel,
+        out_shape=[
+            jax.ShapeDtypeStruct(shape, points.dtype),
+            jax.ShapeDtypeStruct((local_count, 1), jnp.float32),
+        ],
+        in_specs=[pl.BlockSpec(memory_space=pltpu.VMEM)] * 2,
+        out_specs=[pl.BlockSpec(memory_space=pltpu.VMEM)] * 2,
+        scratch_shapes=[pltpu.VMEM(shape, points.dtype), *sum_scratch(shape, points.dtype)],
+        compiler_params=sum_params(collective_id),
+        name="gather_pivots",
+    )(spots[:, None], points)
+    return jnp.concatenate([got[p] for p in range(PIECES)], axis=1), norms[:, 0]
 
 
 def on_device(embeddings, pivots):
@@ -220,16 +280,7 @@
     first_row = lax.axis_index(("rows", "sub")) * local_count
     spots = pivots.reshape(-1) - first_row
     count = spots.shape[0]
-    chosen = (spots[:, None] == lax.iota(jnp.int32, local_count)[None, :]).astype(jnp.bfloat16)
-    pieces = 4
-    step = width // pieces
-    mine = jnp.stack([
-        jnp.dot(chosen, embeddings[:, p * step:(p + 1) * step], preferred_element_type=jnp.float32)
-        .astype(jnp.bfloat16) for p in range(pieces)
-    ])
-    got = group_sum(mine, 0)
-    piv_rows = jnp.concatenate([got[p] for p in range(pieces)], axis=1)
-    norms = squares(embeddings)
+    piv_rows, norms = gather_pivots(spots, embeddings, 0)
     piv_sq = squares(piv_rows)
     tile = kernel_tile(embeddings, norms, piv_rows, piv_sq)
     pivot_gram = kernel_tile(piv_rows, piv_sq, piv_rows, piv_sq)

time: 104 us -> 102 us (0.981)
  matrix products: 8.99 us -> 6.04 us
  local copies, waits for them, and re-layouts: 0.55 us -> 2.38 us
  other arithmetic: 2.66 us -> 1.34 us
    dot_general x4 -> x0, matrix products: 2.92 us -> none  [on_device(): jnp.dot(chosen, embeddings[:, p * step:(p + 1) * step], preferred_element...]
    unnamed x4 -> x7, local copies, waits for them, and re-layouts: 0.14 us -> 1.96 us
    reduce_sum x2 -> x1, other arithmetic: 1.57 us -> 0.29 us  [squares(): return jnp.sum(jnp.square(points.astype(jnp.float32)), axis=1)]
where the time goes in v4:
time: 102 us
  Pallas kernels  92.1 us (90%)
  matrix products  6.04 us (6%)
  local copies, waits for them, and re-layouts  2.38 us (2%)
  other arithmetic  1.34 us (1%)
    pallas_call x2, Pallas kernels, lower_inverse(): pl.pallas_call(inverse_kernel, out_shape=jax.ShapeDtypeStruct(matrix.shap...  39.5 us
    pallas_call x1, Pallas kernels, gather_pivots(): pl.pallas_call(pivot_kernel, out_shape=[jax.ShapeDtypeStruct(shape, point...  28.2 us
    pallas_call x1, Pallas kernels, group_sum(): pl.pallas_call(sum_kernel, out_shape=jax.ShapeDtypeStruct(array.shape, ar...  24.5 us
    dot_general x3, matrix products, exact_dot(): lax.dot_general(first, second, (((first_dim,), (second_dim,)), ((), ())),...  4.76 us

profile of v4, /device:TPU:0, one launch (start us, length us, event | category | flops | bytes accessed | tf_op | source)
XLA Modules:
  0.0 102.1 jit_solution(8894982854085438809)
XLA Ops:
  0.0 0.7 subtract_bitcast_fusion
  0.7 0.1 copy.10
  0.8 0.0 copy-start
  0.9 1.0 %copy-done = bf16[256,1024]{1,0:T(8,128)(2,1)S(1)} copy-done((bf16[256,1024]{1,0:T(8,128)(2,1)S(1)}, bf16[256,1024]{1,0:T(8,128)(2,1)}, u32[]{:S(2)}) %copy-start) | copy-done | bytes 524312
  1.9 28.2 %gather_pivots.1 = (bf16[4,512,256]{2,1,0:T(8,128)(2,1)S(1)}, f32[256,1]{1,0:T(8,128)S(1)}) custom-call(s32[512,1]{1,0:T(8,128)S(1)} %bitcast.34, bf16[256,1024]{1,0:T(8,128)(2,1)S(1)} %copy-done), custom_call_target="tpu_custom_call" | custom-call | tf_op jit(solution)/shard_map/gather_pivots/pallas_call | solution.py:262
  30.1 0.1 slice_bitcast_fusion.7
  30.2 0.0 copy-start.1
  30.2 0.1 reduce
  30.3 0.3 multiply_reduce_fusion
  30.6 0.6 copy-done.1
  31.2 0.5 fusion.7
  31.7 0.8 fusion.3.a_ref
  32.5 19.7 %lower_inverse.2 = f32[512,512]{1,0:T(8,128)S(1)} custom-call(f32[512,512]{1,0:T(8,128)S(1)} %fusion.3.a_ref), custom_call_target="tpu_custom_call" | custom-call | tf_op jit(solution)/shard_map/lower_inverse/pallas_call | solution.py:101
  52.3 1.9 %fusion.9 = f32[256,512]{1,0:T(8,128)S(1)} fusion(f32[512,256]{1,0:T(8,128)S(1)} %fusion.7, f32[512,512]{1,0:T(8,128)S(1)} %lower_inverse.2), kind=kOutput, calls=%fused_computation.29 | convolution fusion | flops 805306368 | bytes 2097152 | tf_op jit(solution)/shard_map/dot_general | solution.py:29
  54.1 1.0 %fusion.10 = f32[512,512]{1,0:T(8,128)S(1)} fusion(f32[256,512]{1,0:T(8,128)S(1)} %fusion.9), kind=kOutput, calls=%fused_computation.30 | convolution fusion | flops 805306368 | bytes 1572864 | tf_op jit(solution)/shard_map/dot_general | solution.py:29
  55.2 0.1 slice_bitcast_fusion.3
  55.2 0.1 pad_maximum_fusion.1.in_ref
  55.3 24.5 %group_sum_1.1 = f32[3,256,256]{2,1,0:T(8,128)S(1)} custom-call(f32[3,256,256]{2,1,0:T(8,128)S(1)} %pad_maximum_fusion.1.in_ref), custom_call_target="tpu_custom_call" | custom-call | tf_op jit(solution)/shard_map/group_sum_1/pallas_call | solution.py:243
  79.8 0.1 broadcast_multiply_fusion
  79.8 0.1 fusion.8
  79.9 0.1 copy.8
  80.1 0.2 copy.7
  80.3 0.1 maximum_add_fusion.a_ref
  80.4 19.8 %lower_inverse.3 = f32[512,512]{1,0:T(8,128)S(1)} custom-call(f32[512,512]{1,0:T(8,128)S(1)} %maximum_add_fusion.a_ref), custom_call_target="tpu_custom_call" | custom-call | tf_op jit(solution)/shard_map/lower_inverse/pallas_call | solution.py:101
  100.2 1.9 %fusion.11 = f32[256,512]{1,0:T(8,128)} fusion(f32[256,512]{1,0:T(8,128)S(1)} %fusion.9, f32[512,512]{1,0:T(8,128)S(1)} %lower_inverse.3), kind=kOutput, calls=%fused_computation.31 | convolution fusion | flops 805306368 | bytes 2097152 | tf_op jit(solution)/shard_map/dot_general | solution.py:29
  (2 shorter events, 0.0 us)
Async XLA Ops:
  0.8 1.0 %copy-start = (bf16[256,1024]{1,0:T(8,128)(2,1)S(1)}, bf16[256,1024]{1,0:T(8,128)(2,1)}, u32[]{:S(2)}) copy-start(bf16[256,1024]{1,0:T(8,128)(2,1)} %points_ref.1) | copy-start | bytes 1572868
  30.2 1.0 %copy-start.1 = (bf16[256,1024]{1,0:T(8,128)(2,1)S(1)}, bf16[256,1024]{1,0:T(8,128)(2,1)}, u32[]{:S(2)}) copy-start(bf16[256,1024]{1,0:T(8,128)(2,1)} %points_ref.1) | copy-start | bytes 1572868

commit v5 on v4

--- a/solution.py
+++ b/solution.py
@@ -209,7 +209,10 @@
         sixth.append(copy)
     for p in range(pieces):
         sixth[p].wait_recv()
-        out_ref[p] = total[p]
+        if before:
+            out_ref[:, p * width:(p + 1) * width] = total[p]
+        else:
+            out_ref[p] = total[p]
     for p in range(pieces):
         for copy in [first[p], second[p], *third[p], *fourth[p], fifth[p], sixth[p]]:
             copy.wait_send()
@@ -262,7 +265,7 @@
     got, norms = pl.pallas_call(
         pivot_kernel,
         out_shape=[
-            jax.ShapeDtypeStruct(shape, points.dtype),
+            jax.ShapeDtypeStruct((count, width), points.dtype),
             jax.ShapeDtypeStruct((local_count, 1), jnp.float32),
         ],
         in_specs=[pl.BlockSpec(memory_space=pltpu.VMEM)] * 2,
@@ -271,7 +274,7 @@
         compiler_params=sum_params(collective_id),
         name="gather_pivots",
     )(spots[:, None], points)
-    return jnp.concatenate([got[p] for p in range(PIECES)], axis=1), norms[:, 0]
+    return got, norms[:, 0]
 
 
 def on_device(embeddings, pivots):
@@ -286,10 +289,16 @@
     pivot_gram = kernel_tile(piv_rows, piv_sq, piv_rows, piv_sq)
     factor = exact_dot(tile, lower_inverse(pivot_gram), 1, 1)
     share = exact_dot(factor, factor, 0, 0)
-    low = count // 2
-    packed = jnp.stack([share[:low, :low], share[low:, :low], share[low:, low:]])
-    packed = group_sum(packed, 1) / (local_count * devices)
-    gram = jnp.block([[packed[0], packed[1].T], [packed[1], packed[2]]])
+    blocks = range(count // TILE)
+    pairs = [(i, j) for i in blocks for j in blocks if i <= j]
+    packed = jnp.concatenate([
+        share[i * TILE:(i + 1) * TILE, j * TILE:(j + 1) * TILE] for i, j in pairs
+    ]).reshape(-1, 2 * TILE, TILE)
+    packed = group_sum(packed, 1).reshape(-1, TILE, TILE) / (local_count * devices)
+    empty = jnp.zeros((TILE, TILE), jnp.float32)
+    gram = jnp.block([
+        [packed[pairs.index((i, j))] if i <= j else empty for j in blocks] for i in blocks
+    ])
     gram = gram + ridge_shift * jnp.eye(count, dtype=jnp.float32)
     return exact_dot(factor, lower_inverse(gram), 1, 1)
 

time: 102 us -> 99.2 us (0.973)
  Pallas kernels: 92.1 us -> 90.2 us
    pallas_call x1, Pallas kernels: 24.5 us -> 22.6 us  [group_sum(): pl.pallas_call(sum_kernel, out_shape=jax.ShapeDtypeStruct(array.shape, ar...]
where the time goes in v5:
time: 99.2 us; the launch traced here: 99 us
  Pallas kernels  90.2 us (91%)
  matrix products  6.06 us (6%)
  local copies, waits for them, and re-layouts  1.36 us (1%)
  other arithmetic  1.19 us (1%)
    pallas_call x2, Pallas kernels, lower_inverse(): pl.pallas_call(inverse_kernel, out_shape=jax.ShapeDtypeStruct(matrix.shap...  39.4 us
    pallas_call x1, Pallas kernels, gather_pivots(): pl.pallas_call(pivot_kernel, out_shape=[jax.ShapeDtypeStruct((count, widt...  28.2 us
    pallas_call x1, Pallas kernels, group_sum(): pl.pallas_call(sum_kernel, out_shape=jax.ShapeDtypeStruct(array.shape, ar...  22.6 us
    dot_general x3, matrix products, exact_dot(): lax.dot_general(first, second, (((first_dim,), (second_dim,)), ((), ())),...  4.76 us

profile of v5, /device:TPU:0, one launch (start us, length us, event | category | flops | bytes accessed | tf_op | source)
XLA Modules:
  0.0 99.0 jit_solution(8088609994183866024)
XLA Ops:
  0.0 0.7 subtract_bitcast_fusion
  0.7 0.1 copy.5
  0.8 0.0 copy-start
  0.9 1.0 %copy-done = bf16[256,1024]{1,0:T(8,128)(2,1)S(1)} copy-done((bf16[256,1024]{1,0:T(8,128)(2,1)S(1)}, bf16[256,1024]{1,0:T(8,128)(2,1)}, u32[]{:S(2)}) %copy-start) | copy-done | bytes 524312
  1.9 0.0 copy-start.1
  1.9 28.2 %gather_pivots.1 = (bf16[512,1024]{1,0:T(8,128)(2,1)S(1)}, f32[256,1]{1,0:T(8,128)S(1)}) custom-call(s32[512,1]{1,0:T(8,128)S(1)} %bitcast.37, bf16[256,1024]{1,0:T(8,128)(2,1)S(1)} %copy-done), custom_call_target="tpu_custom_call" | custom-call | tf_op jit(solution)/shard_map/gather_pivots/pallas_call | solution.py:265
  30.1 0.3 multiply_reduce_fusion
  30.4 0.1 reduce
  30.5 0.0 copy-done.1
  30.5 0.5 fusion.7
  31.0 0.8 fusion.3.a_ref
  31.8 19.7 %lower_inverse.2 = f32[512,512]{1,0:T(8,128)S(1)} custom-call(f32[512,512]{1,0:T(8,128)S(1)} %fusion.3.a_ref), custom_call_target="tpu_custom_call" | custom-call | tf_op jit(solution)/shard_map/lower_inverse/pallas_call | solution.py:101
  51.5 1.9 %fusion.8 = f32[256,512]{1,0:T(8,128)S(1)} fusion(f32[512,256]{1,0:T(8,128)S(1)} %fusion.7, f32[512,512]{1,0:T(8,128)S(1)} %lower_inverse.2), kind=kOutput, calls=%fused_computation.34 | convolution fusion | flops 805306368 | bytes 2097152 | tf_op jit(solution)/shard_map/dot_general | solution.py:29
  53.4 1.0 %fusion.9 = f32[512,512]{1,0:T(8,128)S(1)} fusion(f32[256,512]{1,0:T(8,128)S(1)} %fusion.8), kind=kOutput, calls=%fused_computation.35 | convolution fusion | flops 805306368 | bytes 1572864 | tf_op jit(solution)/shard_map/dot_general | solution.py:29
  54.6 22.6 %group_sum_1.1 = f32[5,256,128]{2,1,0:T(8,128)S(1)} custom-call(f32[5,256,128]{2,1,0:T(8,128)S(1)} %bitcast.38), custom_call_target="tpu_custom_call" | custom-call | tf_op jit(solution)/shard_map/group_sum_1/pallas_call | solution.py:246
  77.3 0.1 maximum_add_fusion.a_ref
  77.4 19.7 %lower_inverse.3 = f32[512,512]{1,0:T(8,128)S(1)} custom-call(f32[512,512]{1,0:T(8,128)S(1)} %maximum_add_fusion.a_ref), custom_call_target="tpu_custom_call" | custom-call | tf_op jit(solution)/shard_map/lower_inverse/pallas_call | solution.py:101
  97.2 1.9 %fusion.10 = f32[256,512]{1,0:T(8,128)} fusion(f32[256,512]{1,0:T(8,128)S(1)} %fusion.8, f32[512,512]{1,0:T(8,128)S(1)} %lower_inverse.3), kind=kOutput, calls=%fused_computation.36 | convolution fusion | flops 805306368 | bytes 2097152 | tf_op jit(solution)/shard_map/dot_general | solution.py:29
  (13 shorter events, 0.2 us)
Async XLA Ops:
  0.8 1.0 %copy-start = (bf16[256,1024]{1,0:T(8,128)(2,1)S(1)}, bf16[256,1024]{1,0:T(8,128)(2,1)}, u32[]{:S(2)}) copy-start(bf16[256,1024]{1,0:T(8,128)(2,1)} %points_ref.1) | copy-start | bytes 1572868
  1.9 28.6 %copy-start.1 = (bf16[256,1024]{1,0:T(8,128)(2,1)S(1)}, bf16[256,1024]{1,0:T(8,128)(2,1)}, u32[]{:S(2)}) copy-start(bf16[256,1024]{1,0:T(8,128)(2,1)} %points_ref.1) | copy-start | bytes 1572868

commit v6 on v5

--- a/solution.py
+++ b/solution.py
@@ -158,19 +158,21 @@
         )
 
     first, second, third, fourth, fifth, sixth = [], [], [], [], [], []
-    for p in range(pieces):
+    def stage_1(p):
         if before and p:
             before(p)
         copy = move(p, 0, in_ref.at[p, cut((1 - core) * n2, n2)], half.at[p], 0)
         copy.start()
         first.append(copy)
-    for p in range(pieces):
+
+    def stage_2(p):
         first[p].wait_recv()
         half[p] = half[p] + in_ref[p, cut(half_at, n2)]
         copy = move(p, 1, half.at[p, cut((1 - x) * n4, n4)], quarter.at[p], 1)
         copy.start()
         second.append(copy)
-    for p in range(pieces):
+
+    def stage_3(p):
         second[p].wait_recv()
         quarter[p] = quarter[p] + half[p, cut(x * n4, n4)]
         copies = []
@@ -179,9 +181,8 @@
             copy.start()
             copies.append(copy)
         third.append(copies)
-    if beside:
-        beside()
-    for p in range(pieces):
+
+    def stage_4(p):
         value = quarter[p, cut(z * n16, n16)]
         for o in (1, 2, 3):
             third[p][o - 1].wait_recv()
@@ -194,25 +195,36 @@
             copy.start()
             copies.append(copy)
         fourth.append(copies)
-    for p in range(pieces):
+
+    def stage_5(p):
         for copy in fourth[p]:
             copy.wait_recv()
         place = total.at[p, cut(quarter_at, n4)]
         copy = move(p, 8, place, place, 1)
         copy.start()
         fifth.append(copy)
-    for p in range(pieces):
+
+    def stage_6(p):
         fifth[p].wait_recv()
         place = total.at[p, cut(half_at, n2)]
         copy = move(p, 9, place, place, 0)
         copy.start()
         sixth.append(copy)
-    for p in range(pieces):
+
+    def stage_7(p):
         sixth[p].wait_recv()
         if before:
             out_ref[:, p * width:(p + 1) * width] = total[p]
         else:
             out_ref[p] = total[p]
+
+    stages = [stage_1, stage_2, stage_3, stage_4, stage_5, stage_6, stage_7]
+    for tick in range(pieces + len(stages) - 1):
+        for level in reversed(range(len(stages))):
+            if 0 <= tick - level < pieces:
+                stages[level](tick - level)
+        if beside and tick == pieces - 1:
+            beside()
     for p in range(pieces):
         for copy in [first[p], second[p], *third[p], *fourth[p], fifth[p], sixth[p]]:
             copy.wait_send()

time: 99.2 us -> 118 us (1.19)
  Pallas kernels: 90.2 us -> 109 us
    pallas_call x1, Pallas kernels: 22.6 us -> 34.5 us  [group_sum(): pl.pallas_call(sum_kernel, out_shape=jax.ShapeDtypeStruct(array.shape, ar...]
    pallas_call x1, Pallas kernels: 28.2 us -> 34.8 us  [gather_pivots(): pl.pallas_call(pivot_kernel, out_shape=[jax.ShapeDtypeStruct((count, widt...]
where the time goes in v6:
time: 118 us
  Pallas kernels  109 us (92%)
  matrix products  6.07 us (5%)
  local copies, waits for them, and re-layouts  1.36 us (1%)
  other arithmetic  1.19 us (1%)
    pallas_call x2, Pallas kernels, lower_inverse(): pl.pallas_call(inverse_kernel, out_shape=jax.ShapeDtypeStruct(matrix.shap...  39.5 us
    pallas_call x1, Pallas kernels, gather_pivots(): pl.pallas_call(pivot_kernel, out_shape=[jax.ShapeDtypeStruct((count, widt...  34.8 us
    pallas_call x1, Pallas kernels, group_sum(): pl.pallas_call(sum_kernel, out_shape=jax.ShapeDtypeStruct(array.shape, ar...  34.5 us
    dot_general x3, matrix products, exact_dot(): lax.dot_general(first, second, (((first_dim,), (second_dim,)), ((), ())),...  4.76 us

profile of v6, /device:TPU:0, one launch (start us, length us, event | category | flops | bytes accessed | tf_op | source)
XLA Modules:
  0.0 117.5 jit_solution(16714081851752822246)
XLA Ops:
  0.0 0.7 subtract_bitcast_fusion
  0.7 0.1 copy.5
  0.8 0.0 copy-start
  0.9 1.0 copy-done
  1.9 0.0 copy-start.1
  1.9 34.8 %gather_pivots.1 = (bf16[512,1024]{1,0:T(8,128)(2,1)S(1)}, f32[256,1]{1,0:T(8,128)S(1)}) custom-call(s32[512,1]{1,0:T(8,128)S(1)} %bitcast.37, bf16[256,1024]{1,0:T(8,128)(2,1)S(1)} %copy-done), custom_call_target="tpu_custom_call" | custom-call | tf_op jit(solution)/shard_map/gather_pivots/pallas_call | solution.py:277
  36.7 0.3 multiply_reduce_fusion
  37.0 0.1 reduce
  37.1 0.0 copy-done.1
  37.1 0.5 fusion.7
  37.6 0.8 fusion.3.a_ref
  38.4 19.7 %lower_inverse.2 = f32[512,512]{1,0:T(8,128)S(1)} custom-call(f32[512,512]{1,0:T(8,128)S(1)} %fusion.3.a_ref), custom_call_target="tpu_custom_call" | custom-call | tf_op jit(solution)/shard_map/lower_inverse/pallas_call | solution.py:101
  58.1 1.9 %fusion.8 = f32[256,512]{1,0:T(8,128)S(1)} fusion(f32[512,256]{1,0:T(8,128)S(1)} %fusion.7, f32[512,512]{1,0:T(8,128)S(1)} %lower_inverse.2), kind=kOutput, calls=%fused_computation.34 | convolution fusion | flops 805306368 | bytes 2097152 | tf_op jit(solution)/shard_map/dot_general | solution.py:29
  60.0 1.0 fusion.9
  61.2 34.5 %group_sum_1.1 = f32[5,256,128]{2,1,0:T(8,128)S(1)} custom-call(f32[5,256,128]{2,1,0:T(8,128)S(1)} %bitcast.38), custom_call_target="tpu_custom_call" | custom-call | tf_op jit(solution)/shard_map/group_sum_1/pallas_call | solution.py:258
  95.8 0.1 maximum_add_fusion.a_ref
  95.9 19.8 %lower_inverse.3 = f32[512,512]{1,0:T(8,128)S(1)} custom-call(f32[512,512]{1,0:T(8,128)S(1)} %maximum_add_fusion.a_ref), custom_call_target="tpu_custom_call" | custom-call | tf_op jit(solution)/shard_map/lower_inverse/pallas_call | solution.py:101
  115.7 1.9 %fusion.10 = f32[256,512]{1,0:T(8,128)} fusion(f32[256,512]{1,0:T(8,128)S(1)} %fusion.8, f32[512,512]{1,0:T(8,128)S(1)} %lower_inverse.3), kind=kOutput, calls=%fused_computation.36 | convolution fusion | flops 805306368 | bytes 2097152 | tf_op jit(solution)/shard_map/dot_general | solution.py:29
  (13 shorter events, 0.2 us)
Async XLA Ops:
  0.8 1.0 copy-start
  1.9 35.2 %copy-start.1 = (bf16[256,1024]{1,0:T(8,128)(2,1)S(1)}, bf16[256,1024]{1,0:T(8,128)(2,1)}, u32[]{:S(2)}) copy-start(bf16[256,1024]{1,0:T(8,128)(2,1)} %points_ref.1) | copy-start | bytes 1572868
